TPU v7x, 32 devices: a whole 2x2x4 slice. The times are simulated.
32 devices in a mesh: grp: 2 (over x), row: 8 (over z, y), col: 2 (over core).
Axes of the slice: x: 2, y: 2, z: 4, core: 2. Of those that a mesh axis runs over, the one named last changes fastest.
Arguments:
- tiles: bfloat16 [1024, 512, 512], P(('grp', 'row', 'col')), parts along dimension 0, may hold values from -0.25 to 0.25
- tile_row: int32 [1024], P(('grp', 'row', 'col')), parts along dimension 0, may hold values from 0 to 31, as said below
- tile_col: int32 [1024], P(('grp', 'row', 'col')), parts along dimension 0, may hold values from 0 to 31, as said below
- counts: int32 [32], P(('grp', 'row', 'col')), parts along dimension 0, may hold values from 10 to 32, as said below
- start: float32 [32768, 64], P(('grp', 'row', 'col')), parts along dimension 0, may hold values from -6 to 6
Outputs:
- basis: float32 [32768, 64], P(('grp', 'row', 'col')), parts along dimension 0
- ritz: float32 [6, 64, 64], P('grp'), parts along dimension 0
There are 2 independent parts, one for each index of `grp`. A program takes and returns all parts, laid end to end along the dimension named above; each array names one. Nothing has to cross between parts.
Inputs may be any that keep to these rules, and one draw needn't show every extreme that they name: `tile_row`: slot s lies on device d = s // 32 = r * 2 + c; its tile row is in r * 2 * 2 to (r + 1) * 2 * 2 - 1, and its tile column j has (j // 2) % 2 == c. `tile_col`: see tile_row for which tile columns a device holds. `counts`: some device is full in every draw.
All inputs are finite; a program needn't handle non-finite values.
Results may differ from a plain program's by a relative error of at most 0.0055.
Values may be sent and summed in bfloat16 or wider, within the bound.
A program may use at most 64 MiB of HBM per device.

v0:
```python
import jax
import jax.numpy as jnp
from jax import lax
from jax.sharding import PartitionSpec as P

TILE = 512
ITERS = 3


def per_device(tiles, tile_row, tile_col, counts, start):
    row_count = lax.axis_size("row")
    col_count = lax.axis_size("col")
    row_here = lax.axis_index("row")
    slot_count = tiles.shape[0]
    blocks_here = start.shape[0] // TILE
    band_tiles = col_count * blocks_here
    nodes = start.shape[0] * row_count * col_count
    width = start.shape[1]
    local_row = tile_row - row_here * band_tiles
    position = tile_col // blocks_here // col_count * blocks_here + tile_col % blocks_here
    live_mask = jnp.arange(slot_count, dtype=jnp.int32) < counts[0]
    basis = start
    quotients = []
    for step in range(ITERS):
        low = basis.astype(jnp.bfloat16)
        whole = lax.all_gather(low, "row", axis=0, tiled=True)
        pieces = whole.reshape(row_count * blocks_here, TILE, width)
        chosen = jnp.take(pieces, position, axis=0)
        products = jnp.einsum("sij,sjk->sik", tiles, chosen, preferred_element_type=jnp.float32)
        placing = (
            (local_row[None, :] == jnp.arange(band_tiles, dtype=jnp.int32)[:, None])
            & live_mask[None, :]
        ).astype(jnp.float32)
        partial_sum = jnp.einsum("ts,sik->tik", placing, products, precision=lax.Precision.HIGHEST)
        flat = partial_sum.reshape(band_tiles * TILE, width)
        image = lax.psum_scatter(flat, "col", scatter_dimension=0, tiled=True)
        gram = (
            lax.psum(jnp.dot(image.T, image, precision=lax.Precision.HIGHEST), ("row", "col"))
            / nodes
        )
        quotient = jnp.dot(basis.T, image, precision=lax.Precision.HIGHEST) / jnp.sqrt(
            jnp.float32(nodes)
        )
        quotients.append(lax.psum(quotient, ("row", "col")))
        lower = jnp.linalg.cholesky(gram)
        basis = jax.scipy.linalg.solve_triangular(lower, image.T, lower=True).T
    stacked = jnp.stack(quotients)
    return (basis, stacked)


def solution(mesh):
    return jax.shard_map(
        per_device,
        mesh=mesh,
        in_specs=(
            P(("grp", "row", "col"), None, None),
            P(("grp", "row", "col")),
            P(("grp", "row", "col")),
            P(("grp", "row", "col")),
            P(("grp", "row", "col"), None),
        ),
        out_specs=(P(("grp", "row", "col"), None), P("grp", None, None)),
        check_vma=False,
    )
```

profile of v0, /device:TPU:0, one launch (start us, length us, event | category | flops | bytes accessed | tf_op | source)
XLA Modules:
  0.0 488.1 jit_solution(11238346172812616601)
XLA Ops:
  7.2 1.6 convert_element_type.18
  8.9 0.0 reduce-scatter.4.cloned.1.call-start
  9.6 0.7 compare_and_fusion
  10.3 0.7 broadcast_subtract_fusion
  10.9 42.8 %all-gather.4.cloned.1.call-done = bf16[8192,64]{0,1:T(8,128)(2,1)} async-done(((bf16[1024,64]{0,1:T(8,128)(2,1)}), bf16[8192,64]{0,1:T(8,128)(2,1)}) %all-gather.4.cloned.1.call-update) | async-done | bytes 1048592 | tf_op jit(solution)/shard_map/all_gather | solution.py:26
  53.7 1.3 copy.67
  55.0 0.7 gather_fusion
  55.7 12.9 %convolution_bitcast_fusion.2 = f32[32,512,64]{1,2,0:T(8,128)} fusion(bf16[32,512,512]{2,1,0:T(8,128)(2,1)} %param.10, bf16[32,512,64]{1,2,0:T(8,128)(2,1)S(1)} %gather_fusion, pred[32]{0:T(512)(128)(4,1)S(1)} %get-tuple-element.15), kind=kOutput, calls=%fused_computation.11 | convolution fusion | flops 1074790400 | bytes 23068704 | tf_op jit(solution)/shard_map/sij,sjk->sik/dot_general | solution.py:29
  68.6 5.8 %fusion.4 = f32[4,512,64]{1,0,2:T(4,128)S(1)} fusion(f32[32,512,64]{1,2,0:T(8,128)} %convolution_bitcast_fusion.2, s32[32]{0:T(128)S(1)} %broadcast_subtract_fusion, pred[32]{0:T(512)(128)(4,1)S(1)} %iota_compare_fusion.3), kind=kOutput, calls=%fused_computation.7 | convolution fusion | flops 50331904 | bytes 4718752 | tf_op jit(solution)/shard_map/ts,sik->tik/dot_general | solution.py:34
  74.3 1.0 copy.53
  75.3 0.0 all-gather.6.cloned.1.call-start
  75.4 6.8 %reduce-scatter.4.cloned.1.call-done = f32[1024,64]{0,1:T(8,128)} async-done(((f32[2048,64]{0,1:T(8,128)}), f32[1024,64]{0,1:T(8,128)}) %reduce-scatter.4.cloned.1.call-update) | async-done | bytes 262160 | tf_op jit(solution)/shard_map/reduce_scatter | solution.py:36
  82.2 1.4 fusion.45
  83.6 61.9 %psum.42 = f32[64,64]{0,1:T(8,128)S(1)} all-reduce(f32[64,64]{0,1:T(8,128)S(1)} %fusion.45), channel_id=1, replica_groups=mesh['grp'=2,'row'=8,'col'=2] {'row','col'}, use_global_device_ids=true, to_apply=%region_1.3 | all-reduce | flops 4096 | bytes 32768 | tf_op jit(solution)/shard_map/psum | solution.py:38
  145.5 0.1 copy.32
  145.6 5.8 %cholesky.59 = f32[64,64]{1,0:T(8,128)S(1)} custom-call(f32[64,64]{1,0:T(8,128)S(1)} %fusion.31), custom_call_target="Cholesky" | custom-call | tf_op jit(solution)/shard_map/jit(cholesky)/cholesky | solution.py:45
  151.5 0.6 compare_reduce_fusion.2
  152.1 0.7 fusion.23
  152.8 4.9 %custom-call.7 = f32[1,64,64]{1,2,0:T(8,128)S(1)} custom-call(f32[1,64,64]{2,1,0:T(8,128)S(1)} %fusion.23), custom_call_target="InvertDiagBlocksLowerTriangular" | custom-call | tf_op jit(solution)/shard_map/jit(_solve_triangular)/triangular_solve | solution.py:46
  157.7 1.4 fusion.21
  159.1 0.7 convert_bitcast_fusion.1
  159.8 0.2 reduce-scatter.6.cloned.1.call-start
  160.0 37.4 %all-gather.6.cloned.1.call-done = bf16[8192,64]{0,1:T(8,128)(2,1)} async-done(((bf16[1024,64]{0,1:T(8,128)(2,1)}), bf16[8192,64]{0,1:T(8,128)(2,1)}) %all-gather.6.cloned.1.call-update) | async-done | bytes 1048592 | tf_op jit(solution)/shard_map/all_gather | solution.py:26
  197.3 1.3 copy.66
  198.7 0.7 gather_fusion.1
  199.4 12.9 %convolution_bitcast_fusion.1 = f32[32,512,64]{1,2,0:T(8,128)} fusion(bf16[32,512,512]{2,1,0:T(8,128)(2,1)} %param.10, bf16[32,512,64]{1,2,0:T(8,128)(2,1)S(1)} %gather_fusion.1, pred[32]{0:T(512)(128)(4,1)S(1)} %get-tuple-element.15), kind=kOutput, calls=%fused_computation.10 | convolution fusion | flops 1074790400 | bytes 23068704 | tf_op jit(solution)/shard_map/sij,sjk->sik/dot_general | solution.py:29
  212.2 5.8 %fusion.2 = f32[4,512,64]{1,0,2:T(4,128)S(1)} fusion(f32[32,512,64]{1,2,0:T(8,128)} %convolution_bitcast_fusion.1, s32[32]{0:T(128)S(1)} %broadcast_subtract_fusion, pred[32]{0:T(512)(128)(4,1)S(1)} %iota_compare_fusion.3), kind=kOutput, calls=%fused_computation.5 | convolution fusion | flops 50331904 | bytes 4718752 | tf_op jit(solution)/shard_map/ts,sik->tik/dot_general | solution.py:34
  218.0 1.0 copy.54
  219.0 0.0 all-gather.8.cloned.1.call-start
  219.0 6.8 %reduce-scatter.6.cloned.1.call-done = f32[1024,64]{0,1:T(8,128)} async-done(((f32[2048,64]{0,1:T(8,128)}), f32[1024,64]{0,1:T(8,128)}) %reduce-scatter.6.cloned.1.call-update) | async-done | bytes 262160 | tf_op jit(solution)/shard_map/reduce_scatter | solution.py:36
  225.8 1.4 fusion.46
  227.2 61.9 %psum.43 = f32[64,64]{0,1:T(8,128)S(1)} all-reduce(f32[64,64]{0,1:T(8,128)S(1)} %fusion.46), channel_id=1, replica_groups=mesh['grp'=2,'row'=8,'col'=2] {'row','col'}, use_global_device_ids=true, to_apply=%region_5.9 | all-reduce | flops 4096 | bytes 32768 | tf_op jit(solution)/shard_map/psum | solution.py:38
  289.2 0.1 copy.36
  289.2 5.9 %cholesky.70 = f32[64,64]{1,0:T(8,128)S(1)} custom-call(f32[64,64]{1,0:T(8,128)S(1)} %fusion.29), custom_call_target="Cholesky" | custom-call | tf_op jit(solution)/shard_map/jit(cholesky)/cholesky | solution.py:45
  295.1 0.6 compare_reduce_fusion.1
  295.8 0.7 fusion.24
  296.4 4.9 %custom-call.8 = f32[1,64,64]{1,2,0:T(8,128)S(1)} custom-call(f32[1,64,64]{2,1,0:T(8,128)S(1)} %fusion.24), custom_call_target="InvertDiagBlocksLowerTriangular" | custom-call | tf_op jit(solution)/shard_map/jit(_solve_triangular)/triangular_solve | solution.py:46
  301.3 1.4 fusion.19
  302.7 0.7 copy-done.2
  303.4 0.7 convert_bitcast_fusion
  304.1 0.3 reduce-scatter.8.cloned.1.call-start
  304.4 37.3 %all-gather.8.cloned.1.call-done = bf16[8192,64]{0,1:T(8,128)(2,1)} async-done(((bf16[1024,64]{0,1:T(8,128)(2,1)}), bf16[8192,64]{0,1:T(8,128)(2,1)}) %all-gather.8.cloned.1.call-update) | async-done | bytes 1048592 | tf_op jit(solution)/shard_map/all_gather | solution.py:26
  341.7 1.3 copy.65
  343.0 0.7 gather_fusion.2
  343.7 12.9 %convolution_bitcast_fusion = f32[32,512,64]{1,2,0:T(8,128)} fusion(bf16[32,512,512]{2,1,0:T(8,128)(2,1)} %param.10, bf16[32,512,64]{1,2,0:T(8,128)(2,1)S(1)} %gather_fusion.2, pred[32]{0:T(512)(128)(4,1)S(1)} %get-tuple-element.15), kind=kOutput, calls=%fused_computation.9 | convolution fusion | flops 1074790400 | bytes 23068704 | tf_op jit(solution)/shard_map/sij,sjk->sik/dot_general | solution.py:29
  356.6 5.9 %fusion = f32[4,512,64]{1,0,2:T(4,128)S(1)} fusion(f32[32,512,64]{1,2,0:T(8,128)} %convolution_bitcast_fusion, s32[32]{0:T(128)S(1)} %broadcast_subtract_fusion, pred[32]{0:T(512)(128)(4,1)S(1)} %iota_compare_fusion.3), kind=kOutput, calls=%fused_computation.3 | convolution fusion | flops 50331904 | bytes 4718752 | tf_op jit(solution)/shard_map/ts,sik->tik/dot_general | solution.py:34
  362.5 1.0 copy.55
  363.4 0.0 all-reduce.3.cloned.1.call-start
  363.5 1.0 fusion.14
  364.5 1.0 fusion.13
  365.4 4.8 reduce-scatter.8.cloned.1.call-done
  370.3 1.9 fusion.12
  372.2 2.0 fusion.47
  374.2 89.7 %all-reduce.3.cloned.1.call-done = (f32[64,64]{0,1:T(8,128)}, f32[1,64,64]{1,2,0:T(8,128)}, f32[1,64,64]{1,2,0:T(8,128)}, f32[1,64,64]{1,2,0:T(8,128)}) async-done(((f32[64,64]{0,1:T(8,128)}, f32[1,64,64]{1,2,0:T(8,128)}, f32[1,64,64]{1,2,0:T(8,128)}, f32[1,64,64]{1,2,0:T(8,128)}), (f32[64,64]{0,1:T(8,128)}, f32[1,64,64]{1,2,0:T(8,128)}, f32[1,64,64]{1,2,0:T(8,128)}, ...) | async-done | bytes 65552 | tf_op jit(solution)/shard_map/psum | solution.py:38
  463.9 0.8 pad_maximum_fusion
  464.7 0.7 copy.44
  465.5 0.8 broadcast_multiply_fusion
  466.2 0.1 copy.40
  466.3 0.8 fusion.27
  467.1 5.8 %cholesky.81 = f32[64,64]{1,0:T(8,128)S(1)} custom-call(f32[64,64]{1,0:T(8,128)S(1)} %fusion.27), custom_call_target="Cholesky" | custom-call | tf_op jit(solution)/shard_map/jit(cholesky)/cholesky | solution.py:45
  473.0 0.6 compare_reduce_fusion
  473.6 0.7 fusion.25
  474.3 4.9 %custom-call.9 = f32[1,64,64]{1,2,0:T(8,128)S(1)} custom-call(f32[1,64,64]{2,1,0:T(8,128)S(1)} %fusion.25), custom_call_target="InvertDiagBlocksLowerTriangular" | custom-call | tf_op jit(solution)/shard_map/jit(_solve_triangular)/triangular_solve | solution.py:46
  479.2 2.1 convolution_bitcast_fusion.3
  (26 shorter events, 0.3 us)
Async XLA Ops:
  7.2 46.5 %all-gather.4.cloned.1.call-start = ((), (), s32[]{:S(2)}) async-start(), calls=%async_computation.3 | async-start | bytes 1179648 | tf_op jit(solution)/shard_map/all_gather | solution.py:26
  8.9 73.3 %reduce-scatter.4.cloned.1.call-start = ((), (), s32[]{:S(2)}) async-start(), calls=%async_computation.4 | async-start | bytes 786432 | tf_op jit(solution)/shard_map/reduce_scatter | solution.py:36
  75.3 122.0 %all-gather.6.cloned.1.call-start = ((), (), s32[]{:S(2)}) async-start(), calls=%async_computation.5 | async-start | bytes 1179648 | tf_op jit(solution)/shard_map/all_gather | solution.py:26
  159.8 66.1 %reduce-scatter.6.cloned.1.call-start = ((), (), s32[]{:S(2)}) async-start(), calls=%async_computation.6 | async-start | bytes 786432 | tf_op jit(solution)/shard_map/reduce_scatter | solution.py:36
  219.0 122.7 %all-gather.8.cloned.1.call-start = ((), (), s32[]{:S(2)}) async-start(), calls=%async_computation.7 | async-start | bytes 1179648 | tf_op jit(solution)/shard_map/all_gather | solution.py:26
  302.7 0.7 copy-start.2
  304.1 66.2 %reduce-scatter.8.cloned.1.call-start = ((), (), s32[]{:S(2)}) async-start(), calls=%async_computation.8 | async-start | bytes 786432 | tf_op jit(solution)/shard_map/reduce_scatter | solution.py:36
  356.6 6.9 %copy-start = (f32[1024,64]{0,1:T(8,128)S(1)}, f32[1024,64]{0,1:T(8,128)}, u32[]{:S(2)}) copy-start(f32[1024,64]{0,1:T(8,128)} %reduce-scatter.4.cloned.1.call-done) | copy-start | bytes 786436
  356.6 6.9 %copy-start.4 = (f32[1024,64]{0,1:T(8,128)S(1)}, f32[1024,64]{0,1:T(8,128)}, u32[]{:S(2)}) copy-start(f32[1024,64]{0,1:T(8,128)} %param.14) | copy-start | bytes 786436
  356.6 7.9 %copy-start.1 = (f32[1024,64]{0,1:T(8,128)S(1)}, f32[1024,64]{0,1:T(8,128)}, u32[]{:S(2)}) copy-start(f32[1024,64]{0,1:T(8,128)} %reduce-scatter.6.cloned.1.call-done) | copy-start | bytes 786436
  356.6 13.7 %copy-start.3 = (f32[64,1024]{1,0:T(8,128)S(1)}, f32[64,1024]{1,0:T(8,128)}, u32[]{:S(2)}) copy-start(f32[64,1024]{1,0:T(8,128)} %copy-done.2) | copy-start | bytes 786436
  363.4 100.5 %all-reduce.3.cloned.1.call-start = ((), (), s32[]{:S(2)}) async-start(), calls=%async_computation.9 | async-start | bytes 262144 | tf_op jit(solution)/shard_map/psum | solution.py:38
Sparse Core Ops, SparseCore 0:
  10.8 42.8 all-gather.3
  75.4 6.6 reduce-scatter.3
  159.9 37.4 all-gather.5
  219.1 6.6 reduce-scatter.5
  304.2 37.4 all-gather.7
  363.6 6.6 reduce-scatter.7
  375.2 88.6 all-reduce.2
where the time goes:
time: 490 us; the launch traced here: 488 us
  waiting for transfers between devices  226 us (46%)
  blocking collectives  124 us (25%)
  matrix products  69.4 us (14%)
  other arithmetic  42.9 us (9%)
  between operations  15 us (3%)
  local copies, waits for them, and re-layouts  10.6 us (2%)
    psum x2, blocking collectives, per_device(): lax.psum(jnp.dot(image.T, image, precision=lax.Precision.HIGHEST), ('row'...  124 us
    all_gather x3, waiting for transfers between devices, per_device(): whole = lax.all_gather(low, 'row', axis=0, tiled=True)  117 us
    psum x1, waiting for transfers between devices, per_device(): lax.psum(jnp.dot(image.T, image, precision=lax.Precision.HIGHEST), ('row'...  89.7 us
    dot_general x3, matrix products, per_device(): jnp.einsum('sij,sjk->sik', tiles, chosen, preferred_element_type=jnp.floa...  38.6 us
    another operation x9, other arithmetic, per_device(): lower = jnp.linalg.cholesky(gram)  19.6 us
    reduce_scatter x3, waiting for transfers between devices, per_device(): image = lax.psum_scatter(flat, 'col', scatter_dimension=0, tiled=True)  18.5 us
    dot_general x3, matrix products, per_device(): jnp.einsum('ts,sik->tik', placing, products, precision=lax.Precision.HIGH...  17.4 us
    another operation x6, other arithmetic, per_device(): basis = jax.scipy.linalg.solve_triangular(lower, image.T, lower=True).T  16.7 us
  transfers between devices with their start and end apart: 7, of which 7 were waited for; matrix products, arithmetic and copies ran while one was open for 1% of the time, Pallas kernels for 0%

commit v1 on v0

v1 whole, which is shorter than its diff:
```python
import functools

import jax
import jax.numpy as jnp
from jax import lax
from jax.experimental import pallas as pl
from jax.experimental.pallas import tpu as pltpu
from jax.sharding import PartitionSpec as P

TILE = 512
ITERS = 3
MESH = pl.DeviceIdType.MESH
EXACT = lax.Precision.HIGHEST
NT = (((1,), (1,)), ((), ()))
LOADS = 4


def pack(square):
    half = square.shape[0] // 2
    return jnp.concatenate([square[:half], square[half:]], axis=1)


def unpack(packed):
    half = packed.shape[1] // 2
    return jnp.concatenate([packed[:, :half], packed[:, half:]], axis=0)


def inverse_factor(gram, work, scale):
    width = gram.shape[0]
    lanes = 2 * width
    rows = lax.broadcasted_iota(jnp.int32, (width, lanes), 0)
    columns = lax.broadcasted_iota(jnp.int32, (width, lanes), 1)
    rows8 = lax.broadcasted_iota(jnp.int32, (8, lanes), 0)
    eye = (rows + width == columns).astype(jnp.float32)
    padded = jnp.concatenate([gram, jnp.zeros_like(gram)], axis=1)
    work[...] = padded + eye

    def body(block, carry):
        whole = work[...]
        first = pl.multiple_of(block * 8, 8)
        here = work[pl.ds(first, 8), :]
        below = rows - first
        cols = [jnp.broadcast_to(whole[:, q : q + 1], (width, lanes)) for q in range(8)]
        cols8 = [jnp.broadcast_to(here[:, q : q + 1], (8, lanes)) for q in range(8)]
        pivots = jnp.ones((8, lanes), jnp.float32)
        for p in range(8):
            inverse = 1.0 / cols8[p][p : p + 1, :]
            pivots = jnp.where(rows8 == p, inverse, pivots)
            factor = jnp.where(below > p, cols[p] * inverse, 0.0)
            factor8 = jnp.where(rows8 > p, cols8[p] * inverse, 0.0)
            pivot_row = here[p : p + 1, :]
            for q in range(p + 1, 8):
                entry = cols8[q][p : p + 1, :]
                cols[q] = cols[q] - factor * entry
                cols8[q] = cols8[q] - factor8 * entry
            here = here - factor8 * pivot_row
            whole = whole - factor * pivot_row
        scale[pl.ds(first, 8), :] = pivots
        work[...] = pltpu.roll(whole, lanes - 8, 1)
        return carry

    lax.fori_loop(0, width // 8, body, 0)
    return (work[...] * jnp.sqrt(scale[...]))[:, :width]


def kernel(
    row_count,
    y_count,
    nodes,
    tiles_hbm,
    row_ref,
    col_ref,
    count_ref,
    start_ref,
    basis_ref,
    ritz_ref,
    tiles,
    gathered,
    partial,
    crossed,
    image,
    iterate,
    core_sum,
    y_sum,
    z_sum,
    rit_core,
    rit_y,
    rit_z,
    work,
    scale,
    load_sem,
    low_recv,
    low_up,
    low_down,
    low_over,
    cross_send,
    cross_recv,
    core_send,
    core_recv,
    y_send,
    y_recv,
    z_send,
    z_recv,
):
    z_count = row_count // y_count
    me = lax.axis_index("row")
    core = lax.axis_index("col")
    here_z = me // y_count
    here_y = me % y_count
    blocks = iterate.shape[0]
    width = iterate.shape[1]
    slots = tiles.shape[0]
    band = partial.shape[0]
    sibling = {"col": 1 - core}
    over = {"row": here_z * y_count + (1 - here_y)}

    chunk = slots // LOADS
    loads = [
        pltpu.make_async_copy(
            tiles_hbm.at[pl.ds(i * chunk, chunk)],
            tiles.at[pl.ds(i * chunk, chunk)],
            load_sem.at[i],
        )
        for i in range(LOADS)
    ]
    for load in loads:
        load.start()

    barrier = pltpu.get_barrier_semaphore()
    pl.semaphore_signal(barrier, inc=1, device_id=sibling, device_id_type=MESH)
    if y_count > 1:
        pl.semaphore_signal(barrier, inc=1, device_id=over, device_id_type=MESH)
    for step in range(1, z_count):
        other = lax.rem(here_z + step, z_count) * y_count + here_y
        pl.semaphore_signal(barrier, inc=1, device_id={"row": other}, device_id_type=MESH)

    for b in range(blocks):
        iterate[b] = start_ref[b * TILE : (b + 1) * TILE, :].T
        gathered[0, me * blocks + b] = iterate[b].astype(jnp.bfloat16)
    pl.semaphore_wait(barrier, z_count - 1 + (1 if y_count > 1 else 0) + 1)

    def low_copy(k, source, send_sem, device_id):
        part = gathered.at[k, pl.ds(source * blocks, blocks)]
        return pltpu.make_async_remote_copy(
            src_ref=part,
            dst_ref=part,
            send_sem=send_sem.at[k, source],
            recv_sem=low_recv.at[k, source],
            device_id=device_id,
            device_id_type=MESH,
        )

    def up(k, source):
        return low_copy(k, source, low_up, {"row": lax.rem(me + y_count, row_count)})

    def down(k, source):
        return low_copy(k, source, low_down, {"row": lax.rem(me - y_count + row_count, row_count)})

    def across(k, source):
        return low_copy(k, source, low_over, over)

    def gather(k):
        not_top = here_z + 1 < z_count
        not_bottom = here_z > 0

        @pl.when(not_top)
        def _():
            up(k, me).start()

        @pl.when(not_bottom)
        def _():
            down(k, me).start()

        if y_count > 1:
            across(k, me).start()
        for step in range(1, z_count):
            lower = me - step * y_count
            upper = me + step * y_count

            @pl.when(here_z - step >= 0)
            def _():
                up(k, lower).wait_recv()

                @pl.when(not_top)
                def _():
                    up(k, lower).start()

                if y_count > 1:
                    across(k, lower).start()

            @pl.when(here_z + step < z_count)
            def _():
                down(k, upper).wait_recv()

                @pl.when(not_bottom)
                def _():
                    down(k, upper).start()

                if y_count > 1:
                    across(k, upper).start()

        if y_count > 1:
            for z in range(z_count):
                across(k, z * y_count + (1 - here_y)).wait_recv()

    def gather_sent(k):
        for z in range(z_count):
            source = z * y_count + here_y
            if y_count > 1:
                across(k, source).wait_send()

            @pl.when((here_z >= z) & (here_z + 1 < z_count))
            def _():
                up(k, source).wait_send()

            @pl.when((here_z <= z) & (here_z > 0))
            def _():
                down(k, source).wait_send()

    def simple_copy(source, target, send_sem, recv_sem, device_id):
        return pltpu.make_async_remote_copy(
            src_ref=source,
            dst_ref=target,
            send_sem=send_sem,
            recv_sem=recv_sem,
            device_id=device_id,
            device_id_type=MESH,
        )

    def core_copy(buffer, index):
        return simple_copy(
            buffer.at[0], buffer.at[1], core_send.at[index], core_recv.at[index], sibling
        )

    def y_copy(buffer, index):
        return simple_copy(buffer.at[0], buffer.at[1], y_send.at[index], y_recv.at[index], over)

    def z_copies(buffer, index, sending):
        copies = []
        for step in range(1, z_count):
            other = lax.rem(here_z + step, z_count)
            slot = here_z if sending else other
            copies.append(
                simple_copy(
                    buffer.at[slot],
                    buffer.at[slot],
                    z_send.at[index, other],
                    z_recv.at[index, slot],
                    {"row": other * y_count + here_y},
                )
            )
        return copies

    def after_core(index, sums, y_buffer, z_buffer):
        core_copy(sums, index).wait()
        total = sums[0] + sums[1]
        if y_count > 1:
            y_buffer[0] = total
            y_copy(y_buffer, index).start()
        else:
            z_buffer[here_z] = total
            for copy in z_copies(z_buffer, index, True):
                copy.start()

    def after_y(index, y_buffer, z_buffer):
        if y_count > 1:
            y_copy(y_buffer, index).wait()
            z_buffer[here_z] = y_buffer[0] + y_buffer[1]
            for copy in z_copies(z_buffer, index, True):
                copy.start()

    def after_z(index, z_buffer):
        for copy in z_copies(z_buffer, index, False):
            copy.wait_recv()
        total = z_buffer[0]
        for z in range(1, z_count):
            total = total + z_buffer[z]
        return total

    def z_sent(index, z_buffer):
        for copy in z_copies(z_buffer, index, True):
            copy.wait_send()

    live = count_ref[0]
    band_first = me * band

    for k in range(ITERS):
        gather(k)
        partial[...] = jnp.zeros_like(partial)

        def multiply(s, carry):
            tile_col = col_ref[s]
            owner = lax.div(lax.div(tile_col, blocks), 2)
            place = owner * blocks + lax.rem(tile_col, blocks)
            product = lax.dot_general(
                gathered[k, place], tiles[s], NT, preferred_element_type=jnp.float32
            )
            mine = jnp.where(s < live, row_ref[s] - band_first, -1)
            for t in range(band):
                weight = jnp.where(mine == t, 1.0, 0.0).astype(jnp.float32)
                partial[t] += product * weight
            return carry

        if k == 0:
            for load in loads:
                load.wait()
        lax.fori_loop(0, slots, multiply, 0, unroll=2)

        cross = simple_copy(
            partial.at[pl.ds((1 - core) * blocks, blocks)],
            crossed.at[k],
            cross_send.at[k],
            cross_recv.at[k],
            sibling,
        )
        cross.start()
        gather_sent(k)
        cross.wait()
        gram = jnp.zeros((width, width), jnp.float32)
        for b in range(blocks):
            image[b] = partial[core * blocks + b] + crossed[k, b]
            gram = gram + lax.dot_general(
                image[b], image[b], NT, precision=EXACT, preferred_element_type=jnp.float32
            )
        core_sum[k, 0] = pack(gram)
        core_copy(core_sum.at[k], k).start()
        quotient = jnp.zeros((width, width), jnp.float32)
        for b in range(blocks):
            quotient = quotient + lax.dot_general(
                iterate[b], image[b], NT, precision=EXACT, preferred_element_type=jnp.float32
            )
        rit_core[0, k] = pack(quotient)
        last = k == ITERS - 1
        if last:
            core_copy(rit_core, ITERS).start()
        after_core(k, core_sum.at[k], y_sum.at[k], z_sum.at[k])
        if last:
            after_core(ITERS, rit_core, rit_y, rit_z)
        after_y(k, y_sum.at[k], z_sum.at[k])
        if last:
            after_y(ITERS, rit_y, rit_z)
        total = after_z(k, z_sum.at[k])
        inverse = inverse_factor(unpack(total) * (1.0 / nodes), work, scale)
        for b in range(blocks):
            fresh = lax.dot_general(
                inverse,
                image[b],
                (((1,), (0,)), ((), ())),
                precision=EXACT,
                preferred_element_type=jnp.float32,
            )
            if last:
                basis_ref[b * TILE : (b + 1) * TILE, :] = fresh.T
            else:
                iterate[b] = fresh
                gathered[k + 1, me * blocks + b] = fresh.astype(jnp.bfloat16)
        z_sent(k, z_sum.at[k])
    total = after_z(ITERS, rit_z)
    z_sent(ITERS, rit_z)
    for k in range(ITERS):
        ritz_ref[k] = unpack(total[k]) * (float(nodes) ** -0.5)


def per_device(tiles, tile_row, tile_col, counts, start):
    row_count = lax.axis_size("row")
    col_count = lax.axis_size("col")
    y_count = 2 if row_count == 8 else 1
    z_count = row_count // y_count
    blocks = start.shape[0] // TILE
    width = start.shape[1]
    nodes = start.shape[0] * row_count * col_count
    half = (width // 2, 2 * width)
    dma = pltpu.SemaphoreType.DMA
    vmem = pl.BlockSpec(memory_space=pltpu.VMEM)
    smem = pl.BlockSpec(memory_space=pltpu.SMEM)
    return pl.pallas_call(
        functools.partial(kernel, row_count, y_count, nodes),
        out_shape=(
            jax.ShapeDtypeStruct(start.shape, jnp.float32),
            jax.ShapeDtypeStruct((ITERS, width, width), jnp.float32),
        ),
        in_specs=[pl.BlockSpec(memory_space=pl.ANY), smem, smem, smem, vmem],
        out_specs=(vmem, vmem),
        scratch_shapes=[
            pltpu.VMEM(tiles.shape, jnp.bfloat16),
            pltpu.VMEM((ITERS, row_count * blocks, width, TILE), jnp.bfloat16),
            pltpu.VMEM((col_count * blocks, width, TILE), jnp.float32),
            pltpu.VMEM((ITERS, blocks, width, TILE), jnp.float32),
            pltpu.VMEM((blocks, width, TILE), jnp.float32),
            pltpu.VMEM((blocks, width, TILE), jnp.float32),
            pltpu.VMEM((ITERS, 2) + half, jnp.float32),
            pltpu.VMEM((ITERS, 2) + half, jnp.float32),
            pltpu.VMEM((ITERS, z_count) + half, jnp.float32),
            pltpu.VMEM((2, ITERS) + half, jnp.float32),
            pltpu.VMEM((2, ITERS) + half, jnp.float32),
            pltpu.VMEM((z_count, ITERS) + half, jnp.float32),
            pltpu.VMEM((width, 2 * width), jnp.float32),
            pltpu.VMEM((width, 2 * width), jnp.float32),
            dma((LOADS,)),
            dma((ITERS, row_count)),
            dma((ITERS, row_count)),
            dma((ITERS, row_count)),
            dma((ITERS, row_count)),
            dma((ITERS,)),
            dma((ITERS,)),
            dma((ITERS + 1,)),
            dma((ITERS + 1,)),
            dma((ITERS + 1,)),
            dma((ITERS + 1,)),
            dma((ITERS + 1, z_count)),
            dma((ITERS + 1, z_count)),
        ],
        compiler_params=pltpu.CompilerParams(
            collective_id=0, has_side_effects=True, vmem_limit_bytes=56 * 1024 * 1024
        ),
    )(tiles, tile_row, tile_col, counts, start)


def solution(mesh):
    return jax.shard_map(
        per_device,
        mesh=mesh,
        in_specs=(
            P(("grp", "row", "col"), None, None),
            P(("grp", "row", "col")),
            P(("grp", "row", "col")),
            P(("grp", "row", "col")),
            P(("grp", "row", "col"), None),
        ),
        out_specs=(P(("grp", "row", "col"), None), P("grp", None, None)),
        check_vma=False,
    )
```

time: 490 us -> 122 us (0.25)
  waiting for transfers between devices: 226 us -> 0 us
  blocking collectives: 124 us -> 0 us
  Pallas kernels: 0 us -> 115 us
  matrix products: 69.4 us -> 0 us
  other arithmetic: 42.9 us -> 0 us
  between operations: 15 us -> 1.29 us
  local copies, waits for them, and re-layouts: 10.6 us -> 5.41 us
    psum x2 -> x0, blocking collectives: 124 us -> none  [per_device(): lax.psum(jnp.dot(image.T, image, precision=lax.Precision.HIGHEST), ('row'...]
    all_gather x3 -> x0, waiting for transfers between devices: 117 us -> none  [per_device(): whole = lax.all_gather(low, 'row', axis=0, tiled=True)]
    pallas_call x0 -> x1, Pallas kernels: none -> 115 us  [per_device(): pl.pallas_call(functools.partial(kernel, row_count, y_count, nodes), out_...]
    psum x1 -> x0, waiting for transfers between devices: 89.7 us -> none  [per_device(): lax.psum(jnp.dot(image.T, image, precision=lax.Precision.HIGHEST), ('row'...]
    dot_general x12 -> x0, matrix products: 64.6 us -> none  [the longest x3 38.6 us: per_device(): jnp.einsum('sij,sjk->sik', tiles, chosen, preferred_element_type=jnp.floa...]
    another operation x16 -> x0, other arithmetic: 37 us -> none  [the longest x9 19.6 us: per_device(): lower = jnp.linalg.cholesky(gram)]
    reduce_scatter x3 -> x0, waiting for transfers between devices: 18.5 us -> none  [per_device(): image = lax.psum_scatter(flat, 'col', scatter_dimension=0, tiled=True)]
  transfers between devices with their start and end apart: 7 -> 0, of which waited for: 7 -> 0; matrix products, arithmetic and copies ran while one was open for 1% -> 0% of each run, Pallas kernels for 0% -> 0%
where the time goes in v1:
time: 122 us
  Pallas kernels  115 us (94%)
  local copies, waits for them, and re-layouts  5.41 us (4%)
  between operations  1.29 us (1%)
    pallas_call x1, Pallas kernels, per_device(): pl.pallas_call(functools.partial(kernel, row_count, y_count, nodes), out_...  115 us
    unnamed x2, local copies, waits for them, and re-layouts  3.48 us

profile of v1, /device:TPU:0, one launch (start us, length us, event | category | flops | bytes accessed | tf_op | source)
XLA Modules:
  0.0 121.9 jit_solution(12315922520385917754)
XLA Ops:
  1.3 1.9 %copy.7.start_ref = f32[1024,64]{1,0:T(8,128)} copy(f32[1024,64]{0,1:T(8,128)} %param.9) | data formatting | bytes 524288 | tf_op args[4]
  3.2 115.2 %shard_map.68 = (f32[1024,64]{1,0:T(8,128)}, f32[3,64,64]{2,1,0:T(8,128)}) custom-call(bf16[32,512,512]{2,1,0:T(8,128)(2,1)} %tiles_hbm.1, s32[32]{0:T(128)} %row_ref.1, s32[32]{0:T(128)} %col_ref.1, s32[1]{0:T(128)S(6)} %copy.10.count_ref, f32[1024,64]{1,0:T(8,128)} %copy.7.start_ref), custom_call_target="tpu_custom_call" | custom-call | tf_op jit(solution)/shard_map/pallas_call | solution.py:376
  118.5 1.9 %copy.8 = f32[1024,64]{0,1:T(8,128)} copy(f32[1024,64]{1,0:T(8,128)} %get-tuple-element.2) | data formatting | bytes 524288 | tf_op jit(solution)/shard_map/pallas_call | solution.py:376
  120.4 1.5 %copy.11 = f32[3,64,64]{2,1,0:T(8,128)} copy(f32[3,64,64]{2,1,0:T(8,128)} %get-tuple-element.7) | data formatting | bytes 98304

commit v2 on v1

v2 whole, which is shorter than its diff:
```python
import functools

import jax
import jax.numpy as jnp
from jax import lax
from jax.experimental import pallas as pl
from jax.experimental.pallas import tpu as pltpu
from jax.sharding import PartitionSpec as P

TILE = 512
ITERS = 3
MESH = pl.DeviceIdType.MESH
EXACT = lax.Precision.HIGHEST
NT = (((1,), (1,)), ((), ()))
LOADS = 4
PARTS = 2
EXTRA = 2


def pack(square):
    half = square.shape[0] // 2
    return jnp.concatenate([square[:half], square[half:]], axis=1)


def unpack(packed):
    half = packed.shape[1] // 2
    return jnp.concatenate([packed[:, :half], packed[:, half:]], axis=0)


def inverse_factor(gram, work, scale):
    width = gram.shape[0]
    lanes = 2 * width
    rows = lax.broadcasted_iota(jnp.int32, (width, lanes), 0)
    columns = lax.broadcasted_iota(jnp.int32, (width, lanes), 1)
    rows8 = lax.broadcasted_iota(jnp.int32, (8, lanes), 0)
    eye = (rows + width == columns).astype(jnp.float32)
    padded = jnp.concatenate([gram, jnp.zeros_like(gram)], axis=1)
    work[...] = padded + eye

    def body(block, carry):
        whole = work[...]
        first = pl.multiple_of(block * 8, 8)
        here = work[pl.ds(first, 8), :]
        below = rows - first
        cols = [jnp.broadcast_to(whole[:, q : q + 1], (width, lanes)) for q in range(8)]
        cols8 = [jnp.broadcast_to(here[:, q : q + 1], (8, lanes)) for q in range(8)]
        pivots = jnp.ones((8, lanes), jnp.float32)
        for p in range(8):
            inverse = 1.0 / cols8[p][p : p + 1, :]
            pivots = jnp.where(rows8 == p, inverse, pivots)
            factor = jnp.where(below > p, cols[p] * inverse, 0.0)
            factor8 = jnp.where(rows8 > p, cols8[p] * inverse, 0.0)
            pivot_row = here[p : p + 1, :]
            for q in range(p + 1, 8):
                entry = cols8[q][p : p + 1, :]
                cols[q] = cols[q] - factor * entry
                cols8[q] = cols8[q] - factor8 * entry
            here = here - factor8 * pivot_row
            whole = whole - factor * pivot_row
        scale[pl.ds(first, 8), :] = pivots
        work[...] = pltpu.roll(whole, lanes - 8, 1)
        return carry

    lax.fori_loop(0, width // 8, body, 0)
    return (work[...] * jnp.sqrt(scale[...]))[:, :width]


def kernel(
    row_count,
    y_count,
    nodes,
    tiles_hbm,
    row_ref,
    col_ref,
    count_ref,
    start_ref,
    basis_ref,
    ritz_ref,
    tiles,
    gathered,
    partial,
    crossed,
    image,
    iterate,
    core_sum,
    row_sum,
    work,
    scale,
    load_sem,
    low_recv,
    low_up,
    low_down,
    low_over,
    cross_send,
    cross_recv,
    core_send,
    core_recv,
    row_send,
    row_recv,
):
    z_count = row_count // y_count
    me = lax.axis_index("row")
    core = lax.axis_index("col")
    here_z = me // y_count
    here_y = me % y_count
    blocks = iterate.shape[0]
    width = iterate.shape[1]
    slots = tiles.shape[0]
    band = partial.shape[0]
    sibling = {"col": 1 - core}
    over = {"row": here_z * y_count + (1 - here_y)}

    chunk = slots // LOADS
    loads = [
        pltpu.make_async_copy(
            tiles_hbm.at[pl.ds(i * chunk, chunk)],
            tiles.at[pl.ds(i * chunk, chunk)],
            load_sem.at[i],
        )
        for i in range(LOADS)
    ]
    for load in loads:
        load.start()

    barrier = pltpu.get_barrier_semaphore()
    pl.semaphore_signal(barrier, inc=1, device_id=sibling, device_id_type=MESH)
    for step in range(1, row_count):
        other = lax.rem(me + step, row_count)
        pl.semaphore_signal(barrier, inc=1, device_id={"row": other}, device_id_type=MESH)

    for b in range(blocks):
        iterate[b] = start_ref[:, b * TILE : (b + 1) * TILE]
        gathered[0, me * blocks + b] = iterate[b].astype(jnp.bfloat16)
    pl.semaphore_wait(barrier, row_count)

    not_top = here_z + 1 < z_count
    not_bottom = here_z > 0

    def at_end(z):
        return y_count > 1 and z in (0, z_count - 1)

    pieces = blocks * PARTS
    piece_rows = width // PARTS

    def low_copy(k, item, send_sem, device_id):
        z, y, q = item
        row = z * y_count + y
        piece = gathered.at[
            k, row * blocks + q // PARTS, pl.ds(q % PARTS * piece_rows, piece_rows)
        ]
        flag = row * pieces + q
        return pltpu.make_async_remote_copy(
            src_ref=piece,
            dst_ref=piece,
            send_sem=send_sem.at[k, flag],
            recv_sem=low_recv.at[k, flag],
            device_id=device_id,
            device_id_type=MESH,
        )

    def up(k, item):
        return low_copy(k, item, low_up, {"row": lax.rem(me + y_count, row_count)})

    def down(k, item):
        return low_copy(k, item, low_down, {"row": lax.rem(me - y_count + row_count, row_count)})

    def across(k, item):
        return low_copy(k, item, low_over, over)

    plain = pieces - EXTRA

    def gather(k):
        for b in reversed(range(pieces)):
            item = (here_z, here_y, b)

            @pl.when(not_top)
            def _():
                up(k, item).start()

            @pl.when(not_bottom)
            def _():
                down(k, item).start()

            if y_count > 1:
                across(k, item).start()

        if y_count > 1:
            for b in reversed(range(plain, pieces)):
                item = (here_z, 1 - here_y, b)

                @pl.when(here_z == 0)
                def _():
                    across(k, item).wait_recv()
                    up(k, item).start()

                @pl.when(here_z == z_count - 1)
                def _():
                    across(k, item).wait_recv()
                    down(k, item).start()

        for step in range(1, z_count):
            lower = here_z - step
            upper = here_z + step
            for b in reversed(range(pieces)):

                @pl.when(lower >= 0)
                def _():
                    item = (lower, here_y, b)
                    up(k, item).wait_recv()

                    @pl.when(not_top)
                    def _():
                        up(k, item).start()

                    if y_count > 1:
                        if b < plain:
                            across(k, item).start()
                        else:

                            @pl.when(lower > 0)
                            def _():
                                across(k, item).start()

                @pl.when(upper < z_count)
                def _():
                    item = (upper, here_y, b)
                    down(k, item).wait_recv()

                    @pl.when(not_bottom)
                    def _():
                        down(k, item).start()

                    if y_count > 1:
                        if b < plain:
                            across(k, item).start()
                        else:

                            @pl.when(upper < z_count - 1)
                            def _():
                                across(k, item).start()

            if y_count > 1:
                for b in reversed(range(plain, pieces)):

                    @pl.when(lower == 0)
                    def _():
                        item = (0, 1 - here_y, b)
                        up(k, item).wait_recv()

                        @pl.when(not_top)
                        def _():
                            up(k, item).start()

                    @pl.when(upper == z_count - 1)
                    def _():
                        item = (z_count - 1, 1 - here_y, b)
                        down(k, item).wait_recv()

                        @pl.when(not_bottom)
                        def _():
                            down(k, item).start()

        if y_count > 1:
            for z in range(z_count):
                for b in range(pieces):
                    if b < plain or not at_end(z):
                        across(k, (z, 1 - here_y, b)).wait_recv()

    def gather_sent(k):
        for z in range(z_count):
            for b in range(pieces):
                item = (z, here_y, b)
                extra = b >= plain and at_end(z)
                if y_count > 1:
                    if extra:

                        @pl.when(here_z == z)
                        def _():
                            across(k, item).wait_send()

                    else:
                        across(k, item).wait_send()

                @pl.when((here_z >= z) & not_top)
                def _():
                    up(k, item).wait_send()
                    if extra:
                        up(k, (z, 1 - here_y, b)).wait_send()

                @pl.when((here_z <= z) & not_bottom)
                def _():
                    down(k, item).wait_send()
                    if extra:
                        down(k, (z, 1 - here_y, b)).wait_send()

    def simple_copy(source, target, send_sem, recv_sem, device_id):
        return pltpu.make_async_remote_copy(
            src_ref=source,
            dst_ref=target,
            send_sem=send_sem,
            recv_sem=recv_sem,
            device_id=device_id,
            device_id_type=MESH,
        )

    def core_copy(i):
        return simple_copy(
            core_sum.at[i, 0], core_sum.at[i, 1], core_send.at[i], core_recv.at[i], sibling
        )

    def row_copies(i, sending):
        copies = []
        for step in range(1, row_count):
            other = lax.rem(me + step, row_count)
            slot = me if sending else other
            copies.append(
                simple_copy(
                    row_sum.at[i, slot],
                    row_sum.at[i, slot],
                    row_send.at[i, other],
                    row_recv.at[i, slot],
                    {"row": other},
                )
            )
        return copies

    def spread(i):
        core_copy(i).wait()
        row_sum[i, me] = core_sum[i, 0] + core_sum[i, 1]
        for copy in row_copies(i, True):
            copy.start()

    def collect(i):
        for copy in row_copies(i, False):
            copy.wait_recv()
        total = row_sum[i, 0]
        for r in range(1, row_count):
            total = total + row_sum[i, r]
        return unpack(total)

    def collect_ritz(k):
        ritz_ref[k] = collect(ITERS + k) * (float(nodes) ** -0.5)

    def row_sent(i):
        for copy in row_copies(i, True):
            copy.wait_send()

    live = count_ref[0]
    band_first = me * band

    for k in range(ITERS):
        gather(k)
        if k > 0:
            spread(ITERS + k - 1)
        partial[...] = jnp.zeros_like(partial)

        def multiply(s, carry):
            tile_col = col_ref[s]
            owner = lax.div(lax.div(tile_col, blocks), 2)
            place = owner * blocks + lax.rem(tile_col, blocks)
            product = lax.dot_general(
                gathered[k, place], tiles[s], NT, preferred_element_type=jnp.float32
            )
            mine = jnp.where(s < live, row_ref[s] - band_first, -1)
            for t in range(band):
                weight = jnp.where(mine == t, 1.0, 0.0).astype(jnp.float32)
                partial[t] += product * weight
            return carry

        if k == 0:
            for load in loads:
                load.wait()
        lax.fori_loop(0, slots, multiply, 0, unroll=4)

        cross = simple_copy(
            partial.at[pl.ds((1 - core) * blocks, blocks)],
            crossed.at[k],
            cross_send.at[k],
            cross_recv.at[k],
            sibling,
        )
        cross.start()
        gather_sent(k)
        if k > 0:
            collect_ritz(k - 1)
            row_sent(ITERS + k - 1)
        cross.wait()
        gram = jnp.zeros((width, width), jnp.float32)
        for b in range(blocks):
            image[b] = partial[core * blocks + b] + crossed[k, b]
            gram = gram + lax.dot_general(
                image[b], image[b], NT, precision=EXACT, preferred_element_type=jnp.float32
            )
        core_sum[k, 0] = pack(gram)
        core_copy(k).start()
        quotient = jnp.zeros((width, width), jnp.float32)
        for b in range(blocks):
            quotient = quotient + lax.dot_general(
                iterate[b], image[b], NT, precision=EXACT, preferred_element_type=jnp.float32
            )
        core_sum[ITERS + k, 0] = pack(quotient)
        last = k == ITERS - 1
        core_copy(ITERS + k).start()
        spread(k)
        if last:
            spread(ITERS + k)
        inverse = inverse_factor(collect(k) * (1.0 / nodes), work, scale)
        for b in range(blocks):
            fresh = lax.dot_general(
                inverse,
                image[b],
                (((1,), (0,)), ((), ())),
                precision=EXACT,
                preferred_element_type=jnp.float32,
            )
            if last:
                basis_ref[:, b * TILE : (b + 1) * TILE] = fresh
            else:
                iterate[b] = fresh
                gathered[k + 1, me * blocks + b] = fresh.astype(jnp.bfloat16)
        row_sent(k)
    collect_ritz(ITERS - 1)
    row_sent(2 * ITERS - 1)


def per_device(tiles, tile_row, tile_col, counts, start):
    row_count = lax.axis_size("row")
    col_count = lax.axis_size("col")
    y_count = 2 if row_count == 8 else 1
    z_count = row_count // y_count
    blocks = start.shape[0] // TILE
    width = start.shape[1]
    nodes = start.shape[0] * row_count * col_count
    half = (width // 2, 2 * width)
    dma = pltpu.SemaphoreType.DMA
    vmem = pl.BlockSpec(memory_space=pltpu.VMEM)
    smem = pl.BlockSpec(memory_space=pltpu.SMEM)
    basis, ritz = pl.pallas_call(
        functools.partial(kernel, row_count, y_count, nodes),
        out_shape=(
            jax.ShapeDtypeStruct((width, start.shape[0]), jnp.float32),
            jax.ShapeDtypeStruct((ITERS, width, width), jnp.float32),
        ),
        in_specs=[pl.BlockSpec(memory_space=pl.ANY), smem, smem, smem, vmem],
        out_specs=(vmem, vmem),
        scratch_shapes=[
            pltpu.VMEM(tiles.shape, jnp.bfloat16),
            pltpu.VMEM((ITERS, row_count * blocks, width, TILE), jnp.bfloat16),
            pltpu.VMEM((col_count * blocks, width, TILE), jnp.float32),
            pltpu.VMEM((ITERS, blocks, width, TILE), jnp.float32),
            pltpu.VMEM((blocks, width, TILE), jnp.float32),
            pltpu.VMEM((blocks, width, TILE), jnp.float32),
            pltpu.VMEM((2 * ITERS, 2) + half, jnp.float32),
            pltpu.VMEM((2 * ITERS, row_count) + half, jnp.float32),
            pltpu.VMEM((width, 2 * width), jnp.float32),
            pltpu.VMEM((width, 2 * width), jnp.float32),
            dma((LOADS,)),
            dma((ITERS, row_count * blocks * PARTS)),
            dma((ITERS, row_count * blocks * PARTS)),
            dma((ITERS, row_count * blocks * PARTS)),
            dma((ITERS, row_count * blocks * PARTS)),
            dma((ITERS,)),
            dma((ITERS,)),
            dma((2 * ITERS,)),
            dma((2 * ITERS,)),
            dma((2 * ITERS, row_count)),
            dma((2 * ITERS, row_count)),
        ],
        compiler_params=pltpu.CompilerParams(
            collective_id=0, has_side_effects=True, vmem_limit_bytes=56 * 1024 * 1024
        ),
    )(tiles, tile_row, tile_col, counts, start.T)
    return basis.T, ritz


def solution(mesh):
    return jax.shard_map(
        per_device,
        mesh=mesh,
        in_specs=(
            P(("grp", "row", "col"), None, None),
            P(("grp", "row", "col")),
            P(("grp", "row", "col")),
            P(("grp", "row", "col")),
            P(("grp", "row", "col"), None),
        ),
        out_specs=(P(("grp", "row", "col"), None), P("grp", None, None)),
        check_vma=False,
    )
```

time: 122 us -> 110 us (0.902)
  Pallas kernels: 115 us -> 105 us
  local copies, waits for them, and re-layouts: 5.41 us -> 3.21 us
    pallas_call x1, Pallas kernels: 115 us -> 105 us  [per_device(): pl.pallas_call(functools.partial(kernel, row_count, y_count, nodes), out_...]
    pallas_call x1 -> x0, local copies, waits for them, and re-layouts: 1.93 us -> none  [per_device(): pl.pallas_call(functools.partial(kernel, row_count, y_count, nodes), out_...]
where the time goes in v2:
time: 110 us
  Pallas kernels  105 us (95%)
  local copies, waits for them, and re-layouts  3.21 us (3%)
  between operations  1.29 us (1%)
    pallas_call x1, Pallas kernels, per_device(): pl.pallas_call(functools.partial(kernel, row_count, y_count, nodes), out_...  105 us
    unnamed x2, local copies, waits for them, and re-layouts  3.21 us

profile of v2, /device:TPU:0, one launch (start us, length us, event | category | flops | bytes accessed | tf_op | source)
XLA Modules:
  0.0 109.8 jit_solution(13399037698451957946)
XLA Ops:
  1.3 105.3 %shard_map.68 = (f32[64,1024]{1,0:T(8,128)}, f32[3,64,64]{2,1,0:T(8,128)}) custom-call(bf16[32,512,512]{2,1,0:T(8,128)(2,1)} %tiles_hbm.1, s32[32]{0:T(128)} %row_ref.1, s32[32]{0:T(128)} %col_ref.1, s32[1]{0:T(128)S(6)} %copy.9.count_ref, f32[64,1024]{1,0:T(8,128)} %bitcast.2), custom_call_target="tpu_custom_call" | custom-call | tf_op jit(solution)/shard_map/pallas_call | solution.py:438
  106.6 1.7 %copy.10 = f32[1024,64]{0,1:T(8,128)} copy(f32[1024,64]{0,1:T(8,128)} %bitcast.3) | data formatting | bytes 524288
  108.3 1.5 %copy.11 = f32[3,64,64]{2,1,0:T(8,128)} copy(f32[3,64,64]{2,1,0:T(8,128)} %get-tuple-element.9) | data formatting | bytes 98304

commit v3 on v2

--- a/solution.py
+++ b/solution.py
@@ -370,7 +370,7 @@
         if k == 0:
             for load in loads:
                 load.wait()
-        lax.fori_loop(0, slots, multiply, 0, unroll=4)
+        lax.fori_loop(0, slots, multiply, 0, unroll=8)
 
         cross = simple_copy(
             partial.at[pl.ds((1 - core) * blocks, blocks)],

time: 110 us -> 108 us (0.982)
    pallas_call x1, Pallas kernels: 105 us -> 104 us  [per_device(): pl.pallas_call(functools.partial(kernel, row_count, y_count, nodes), out_...]
where the time goes in v3:
time: 108 us
  Pallas kernels  104 us (96%)
  local copies, waits for them, and re-layouts  3.21 us (3%)
  between operations  1.29 us (1%)
    pallas_call x1, Pallas kernels, per_device(): pl.pallas_call(functools.partial(kernel, row_count, y_count, nodes), out_...  104 us
    unnamed x2, local copies, waits for them, and re-layouts  3.21 us

profile of v3, /device:TPU:0, one launch (start us, length us, event | category | flops | bytes accessed | tf_op | source)
XLA Modules:
  0.0 108.0 jit_solution(2867839140654194956)
XLA Ops:
  1.3 103.5 %shard_map.68 = (f32[64,1024]{1,0:T(8,128)}, f32[3,64,64]{2,1,0:T(8,128)}) custom-call(bf16[32,512,512]{2,1,0:T(8,128)(2,1)} %tiles_hbm.1, s32[32]{0:T(128)} %row_ref.1, s32[32]{0:T(128)} %col_ref.1, s32[1]{0:T(128)S(6)} %copy.9.count_ref, f32[64,1024]{1,0:T(8,128)} %bitcast.2), custom_call_target="tpu_custom_call" | custom-call | tf_op jit(solution)/shard_map/pallas_call | solution.py:438
  104.8 1.7 %copy.10 = f32[1024,64]{0,1:T(8,128)} copy(f32[1024,64]{0,1:T(8,128)} %bitcast.3) | data formatting | bytes 524288
  106.5 1.5 %copy.11 = f32[3,64,64]{2,1,0:T(8,128)} copy(f32[3,64,64]{2,1,0:T(8,128)} %get-tuple-element.9) | data formatting | bytes 98304
